TPU v7x, 32 devices: a whole 2x2x4 slice. The times are simulated.
32 devices in a mesh: ha: 4 (over y, x), wa: 8 (over z, core).
Axes of the slice: x: 2, y: 2, z: 4, core: 2. Of those that a mesh axis runs over, the one named last changes fastest.
Arguments:
- features: bfloat16 [4, 128, 256, 192], P(None, 'ha', 'wa'), may hold values from -6 to 6
- conv_first: bfloat16 [3, 3, 3, 192, 192], replicated, may hold values from -0.078125 to 0.078125
- bias_first: float32 [192], replicated, may hold values from -3 to 3
- gain_first: float32 [192], replicated, may hold values from 0.5 to 2
- conv_second: bfloat16 [3, 3, 3, 192, 192], replicated, may hold values from -0.078125 to 0.078125
- gain_second: float32 [192], replicated, may hold values from 0.5 to 2
- up_weight: bfloat16 [3, 3, 192, 96], replicated, may hold values from -0.15625 to 0.15625
- cotangent: bfloat16 [4, 256, 512, 96], P(None, 'ha', 'wa'), may hold values from -6 to 6
Outputs:
- feature_grad: bfloat16 [4, 128, 256, 192], P(None, 'ha', 'wa')
All inputs are finite; a program needn't handle non-finite values.
Results may differ from a plain program's by a relative error of at most 0.0051.
Values may be sent and summed in bfloat16 or wider, within the bound.
A program may use at most 192 MiB of HBM per device.

v0:
```python
import functools

import jax
import jax.numpy as jnp
from jax import lax
from jax.experimental import pallas as pl
from jax.experimental.pallas import tpu as pltpu
from jax.sharding import PartitionSpec as P

MESH = pl.DeviceIdType.MESH
F32, BF16 = jnp.float32, jnp.bfloat16
LEAD = 8
STEP = 8


def rms_scale(value):
    return lax.rsqrt(jnp.mean(value * value, axis=-1, keepdims=True) + 1e-06)


def silu_slope(value):
    sig = jax.nn.sigmoid(value)
    return sig * (1.0 + value * (1.0 - sig))


def rms_back(value, scale, gain, grad):
    scaled = gain * grad
    return scale * scaled - value * scale**3 * jnp.mean(value * scaled, axis=-1, keepdims=True)


class Field:
    def __init__(self, ref, parts, one_frame, rows, cols, pitch):
        self.ref, self.parts, self.one_frame = ref, parts, one_frame
        self.rows, self.cols, self.pitch = rows, cols, pitch

    def part(self, t, h):
        return h if self.one_frame else t * self.parts + h

    def cells(self, t, at):
        return jnp.concatenate([self.ref[self.part(t, h), at, :] for h in range(self.parts)], axis=1)

    def line(self, row):
        return pl.ds(pl.multiple_of(row * self.pitch + LEAD, 8), self.cols)

    def put(self, t, row, values):
        n = self.cols
        for h in range(self.parts):
            for r in range(values.shape[0] // n):
                self.ref[self.part(t, h), self.line(row + r + 1), :] = values[
                    r * n : (r + 1) * n, h * 128 : (h + 1) * 128
                ]

    def get(self, t, row, count):
        return jnp.concatenate([self.cells(t, self.line(row + r + 1)) for r in range(count)], axis=0)

    def column(self, col):
        return pl.ds(self.pitch + LEAD + col, self.rows, stride=self.pitch)

    def take_edges(self, t, stage):
        n = self.cols
        stage[0, t] = self.cells(t, pl.ds(self.pitch + LEAD, n)).astype(BF16)
        stage[1, t] = self.cells(t, pl.ds(self.rows * self.pitch + LEAD, n)).astype(BF16)
        stage[2, t] = self.cells(t, self.column(0)).astype(BF16)
        stage[3, t] = self.cells(t, self.column(n - 1)).astype(BF16)

    def set_edges(self, t, hal, cor, inside):
        up, down, left, right = inside
        n, low = self.cols, (self.rows + 1) * self.pitch + LEAD
        places = [
            (pl.ds(LEAD, n), hal[0, t].astype(F32) * up),
            (pl.ds(low, n), hal[1, t].astype(F32) * down),
            (self.column(-1), hal[2, t].astype(F32) * left),
            (self.column(n), hal[3, t].astype(F32) * right),
            (pl.ds(LEAD - 1, 1), cor[0, t].astype(F32)[15:16] * (up * left)),
            (pl.ds(LEAD + n, 1), cor[1, t].astype(F32)[0:1] * (up * right)),
            (pl.ds(low - 1, 1), cor[2, t].astype(F32)[15:16] * (down * left)),
            (pl.ds(low + n, 1), cor[3, t].astype(F32)[0:1] * (down * right)),
        ]
        for at, values in places:
            for h in range(self.parts):
                self.ref[self.part(t, h), at, :] = values[:, h * 128 : (h + 1) * 128]


def kernel(
    dims, feats, cot, bias_first, gain_first, gain_second, wu, w1_hbm, w2_hbm, w3_hbm, out,
    g0, g1, x0, x1, cf, pre, w1, w2, w3, stage, hal, cor, cstage, chal, ccor,
    w_sem, send, recv,
):
    count_h, count_w, frames, rows, cols, chans, fine_chans = dims
    me_h, me_w = lax.axis_index("ha"), lax.axis_index("wa")
    up, down = lax.rem(me_h + count_h - 1, count_h), lax.rem(me_h + 1, count_h)
    left, right = lax.rem(me_w + count_w - 1, count_w), lax.rem(me_w + 1, count_w)
    inside = [
        jnp.where(has, 1.0, 0.0).astype(F32)
        for has in (me_h > 0, me_h < count_h - 1, me_w > 0, me_w < count_w - 1)
    ]
    peers = [
        (up, me_w), (down, me_w), (me_h, left), (me_h, right),
        (up, left), (up, right), (down, left), (down, right),
    ]
    barrier = pltpu.get_barrier_semaphore()
    for peer in peers:
        pl.semaphore_signal(barrier, inc=1, device_id=peer, device_id_type=MESH)

    loads = [
        pltpu.make_async_copy(src, dst, w_sem.at[i])
        for i, (src, dst) in enumerate(((w1_hbm, w1), (w2_hbm, w2), (w3_hbm, w3)))
    ]
    for load in loads:
        load.start()

    def exchange(stage, hal, cor, sem, t=None):
        at = (slice(None),) if t is None else (t,)
        n = stage.shape[2]
        first, last = pl.ds(0, 16), pl.ds(n - 16, 16)
        routes = [
            (stage.at[(0, *at)], hal.at[(1, *at)]),
            (stage.at[(1, *at)], hal.at[(0, *at)]),
            (stage.at[(2, *at)], hal.at[(3, *at)]),
            (stage.at[(3, *at)], hal.at[(2, *at)]),
            (stage.at[(0, *at, first)], cor.at[(3, *at)]),
            (stage.at[(0, *at, last)], cor.at[(2, *at)]),
            (stage.at[(1, *at, first)], cor.at[(1, *at)]),
            (stage.at[(1, *at, last)], cor.at[(0, *at)]),
        ]
        copies = [
            pltpu.make_async_remote_copy(
                src_ref=src, dst_ref=dst, send_sem=send.at[sem, i], recv_sem=recv.at[sem, i],
                device_id=peer, device_id_type=MESH,
            )
            for i, ((src, dst), peer) in enumerate(zip(routes, peers))
        ]
        for copy in copies:
            copy.start()
        return copies

    def arrive(copies):
        for copy in copies:
            copy.wait()

    pitch = cols + 16
    active = Field(g0, 2, False, rows, cols, pitch)
    block = Field(g1, 2, False, rows, cols, pitch)
    fine = Field(cf, 1, True, 2 * rows, 2 * cols, 2 * cols + 16)
    span = STEP * cols
    steps = rows // STEP

    def over_rows(body):
        @pl.loop(0, steps)
        def _(c):
            body(c * STEP, pl.ds(pl.multiple_of(c * span, span), span))

    zero_lanes = jnp.zeros((2 * cols, 128 - fine_chans), F32)

    def load_fine(t):
        @pl.loop(0, 2 * rows)
        def _(y):
            cells = cot[t, pl.ds(pl.multiple_of(y * 2 * cols, 2 * cols), 2 * cols), :].astype(F32)
            fine.put(t, y, jnp.concatenate([cells, zero_lanes], axis=1))

    for t in range(frames):
        load_fine(t)
        fine.take_edges(t, cstage)
    pl.semaphore_wait(barrier, len(peers))
    cot_sent = exchange(cstage, chal, ccor, 0)

    def pad_lanes(values):
        return jnp.concatenate([values, jnp.zeros((values.shape[0], 256 - chans), F32)], axis=1)

    for t in range(frames):
        def first_norm(row, at, t=t):
            value = feats[t, at, :].astype(F32)
            normed = value * rms_scale(value) * gain_first[...]
            active.put(t, row, pad_lanes(normed * jax.nn.sigmoid(normed)))
        over_rows(first_norm)
        active.take_edges(t, stage.at[0])
    active_sent = exchange(stage.at[0], hal.at[0], cor.at[0], 1)

    arrive(cot_sent)
    for t in range(frames):
        load_fine(t)
        fine.set_edges(t, chal, ccor, inside)

        def coarse(row, at, t=t):
            def pairs(y):
                base = y * fine.pitch + LEAD
                before, even, odd, after = [
                    cf[0, pl.ds(base + d, cols, stride=2), :] for d in (-1, 0, 1, 2)
                ]
                return [before + even, even + odd, odd + after]

            taps = [[] for _ in range(9)]
            ahead = pairs(2 * row)
            for r in range(STEP):
                sums = [ahead] + [pairs(2 * (row + r) + d) for d in (1, 2, 3)]
                ahead = sums[2]
                for a in range(3):
                    for b in range(3):
                        taps[3 * a + b].append((sums[a][b] + sums[a + 1][b]).astype(BF16))
            lhs = jnp.concatenate([jnp.concatenate(tap, axis=0) for tap in taps], axis=1)
            block.put(t, row, pad_lanes(jnp.dot(lhs, wu[...], preferred_element_type=F32)))

        over_rows(coarse)
        block.take_edges(t, stage.at[1])
    block_sent = exchange(stage.at[1], hal.at[1], cor.at[1], 2)

    def widen(field, t, x):
        gap = jnp.zeros((cols, x.shape[-1] - 3 * chans), F32)

        @pl.loop(0, rows + 2)
        def _(row):
            line = field.cells(t, pl.ds(pl.multiple_of(row * pitch, 16), pitch))
            cells = [line[LEAD + d : LEAD + d + cols, :chans] for d in (-1, 0, 1)]
            x[t, pl.ds(pl.multiple_of(row * cols, cols), cols), :] = jnp.concatenate([*cells, gap], axis=1).astype(BF16)

    def conv(x, weight, sources, row):
        total = None
        for k, t in sources:
            lhs = jnp.concatenate(
                [x[t, pl.ds(pl.multiple_of((row + p) * cols, cols), span), :] for p in range(3)], axis=1
            )
            part = jnp.dot(lhs, weight[k], preferred_element_type=F32)
            total = part if total is None else total + part
        return total

    arrive(active_sent)
    loads[0].wait()
    for t in range(frames):
        active.set_edges(t, hal.at[0], cor.at[0], inside)
        widen(active, t, x0)

        def first_conv(row, at, t=t):
            sources = [(k, t - 2 + k) for k in range(3) if t - 2 + k >= 0]
            pre[t, at, :] = conv(x0, w1, sources, row) + bias_first[...]

        over_rows(first_conv)

    later = lambda t: [(j, t + j) for j in range(3) if t + j < frames]
    arrive(block_sent)
    loads[1].wait()
    pre_sent = [None] * frames
    for t in reversed(range(frames)):
        block.set_edges(t, hal.at[1], cor.at[1], inside)
        widen(block, t, x1)

        def second_conv(row, at, t=t):
            value = pre[t, at, :]
            scale = rms_scale(value)
            grad = conv(x1, w2, later(t), row) * silu_slope(value * scale * gain_second[...])
            active.put(t, row, pad_lanes(rms_back(value, scale, gain_second[...], grad)))

        over_rows(second_conv)
        active.take_edges(t, stage.at[2])
        pre_sent[t] = exchange(stage.at[2], hal.at[2], cor.at[2], 3 + t, t)

    loads[2].wait()
    for t in reversed(range(frames)):
        arrive(pre_sent[t])
        active.set_edges(t, hal.at[2], cor.at[2], inside)
        widen(active, t, x0)

        def third_conv(row, at, t=t):
            value = feats[t, at, :].astype(F32)
            scale = rms_scale(value)
            grad = conv(x0, w3, later(t), row) * silu_slope(value * scale * gain_first[...])
            through = rms_back(value, scale, gain_first[...], grad)
            out[t, at, :] = (block.get(t, row, STEP)[:, :chans] + through).astype(BF16)

        over_rows(third_conv)


def per_device(
    count_h, count_w, features, conv_first, bias_first, gain_first, conv_second, gain_second, up_weight, cotangent
):
    frames, rows, cols, chans = features.shape
    fine_chans = cotangent.shape[-1]
    wide = -(-3 * chans // 128) * 128

    def taps(weight):
        weight = weight.reshape(3, 3, 3 * chans, chans)
        weight = jnp.pad(weight, ((0, 0), (0, 0), (0, wide - 3 * chans), (0, 0)))
        return weight.reshape(3, 3 * wide, chans)

    flip = lambda w: jnp.flip(w, (0, 1, 2)).swapaxes(3, 4)
    up_flip = jnp.pad(jnp.flip(up_weight, (0, 1)).swapaxes(2, 3), ((0, 0), (0, 0), (0, 128 - fine_chans), (0, 0)))
    pitch, fine_pitch = cols + 16, 2 * cols + 16
    vmem, hbm = pl.BlockSpec(memory_space=pltpu.VMEM), pl.BlockSpec(memory_space=pl.ANY)
    dims = (count_h, count_w, frames, rows, cols, chans, fine_chans)
    field = pltpu.VMEM((2 * frames, (rows + 2) * pitch, 128), F32)
    spread = pltpu.VMEM((frames, (rows + 2) * cols, wide), BF16)
    weights = pltpu.VMEM((3, 3 * wide, chans), BF16)
    out = pl.pallas_call(
        functools.partial(kernel, dims),
        out_shape=jax.ShapeDtypeStruct((frames, rows * cols, chans), BF16),
        in_specs=[vmem] * 6 + [hbm] * 3,
        out_specs=vmem,
        scratch_shapes=[
            field, field, spread, spread,
            pltpu.VMEM((1, (2 * rows + 2) * fine_pitch, 128), F32),
            pltpu.VMEM((frames, rows * cols, chans), F32),
            weights, weights, weights,
            pltpu.VMEM((3, 4, frames, cols, 256), BF16),
            pltpu.VMEM((3, 4, frames, cols, 256), BF16),
            pltpu.VMEM((3, 4, frames, 16, 256), BF16),
            pltpu.VMEM((4, frames, 2 * cols, 128), BF16),
            pltpu.VMEM((4, frames, 2 * cols, 128), BF16),
            pltpu.VMEM((4, frames, 16, 128), BF16),
            pltpu.SemaphoreType.DMA((3,)),
            pltpu.SemaphoreType.DMA((3 + frames, 8)),
            pltpu.SemaphoreType.DMA((3 + frames, 8)),
        ],
        compiler_params=pltpu.CompilerParams(
            collective_id=0, has_side_effects=True, vmem_limit_bytes=60 * 2**20
        ),
    )(
        features.reshape(frames, rows * cols, chans),
        cotangent.reshape(frames, 4 * rows * cols, fine_chans),
        bias_first[None], gain_first[None], gain_second[None],
        up_flip.reshape(9 * 128, chans),
        taps(conv_first), taps(flip(conv_second)), taps(flip(conv_first)),
    )
    return out.reshape(frames, rows, cols, chans)


def solution(mesh):
    placed = (P(None, "ha", "wa", None), P(), P(), P(), P(), P(), P(), P(None, "ha", "wa", None))
    body = functools.partial(per_device, mesh.shape["ha"], mesh.shape["wa"])
    return jax.shard_map(body, mesh=mesh, in_specs=placed, out_specs=P(None, "ha", "wa", None), check_vma=False)
```

profile of v0, /device:TPU:0, one launch (start us, length us, event | category | flops | bytes accessed | tf_op | source)
XLA Modules:
  0.0 126.2 jit_solution(9528727817513541905)
XLA Ops:
  0.0 1.0 reverse_bitcast_fusion.2
  1.0 0.2 copy.13
  1.3 0.9 pad.14.clone
  2.2 1.9 %reverse_bitcast_fusion.1 = bf16[3,3,3,192,192]{3,4,2,1,0:T(8,128)(2,1)S(1)} fusion(bf16[3,3,3,192,192]{4,3,2,1,0:T(8,128)(2,1)} %param.12), kind=kLoop, calls=%fused_computation.1 | loop fusion | bytes 3981312 | tf_op jit(solution)/shard_map/transpose | solution.py:283
  4.1 3.6 %copy.11 = bf16[3,3,3,192,192]{4,3,2,1,0:T(8,128)(2,1)} copy(bf16[3,3,3,192,192]{3,4,2,1,0:T(8,128)(2,1)S(1)} %reverse_bitcast_fusion.1) | data formatting | bytes 3981312 | tf_op jit(solution)/shard_map/transpose | solution.py:283
  7.7 0.0 copy-start
  7.7 4.0 %pad.16 = bf16[3,3,640,192]{3,2,1,0:T(8,128)(2,1)} pad(bf16[3,3,576,192]{3,2,1,0:T(8,128)(2,1)} %bitcast.23, bf16[]{:T(256)} %constant.2.clone.1), padding=0_0x0_0x0_64x0_0 | pad | bytes 4202498 | tf_op jit(solution)/shard_map/jit(_pad)/pad | solution.py:280
  11.7 0.0 copy-done
  11.7 0.3 reverse_bitcast_fusion
  11.9 3.6 %copy.12 = bf16[3,3,3,192,192]{4,3,2,1,0:T(8,128)(2,1)} copy(bf16[3,3,3,192,192]{3,4,2,1,0:T(8,128)(2,1)S(1)} %reverse_bitcast_fusion) | data formatting | bytes 3981312 | tf_op jit(solution)/shard_map/transpose | solution.py:283
  15.5 0.0 copy-start.1
  15.5 4.0 %pad.17 = bf16[3,3,640,192]{3,2,1,0:T(8,128)(2,1)} pad(bf16[3,3,576,192]{3,2,1,0:T(8,128)(2,1)} %bitcast.24, bf16[]{:T(256)} %constant.2.clone.1), padding=0_0x0_0x0_64x0_0 | pad | bytes 4202498 | tf_op jit(solution)/shard_map/jit(_pad)/pad | solution.py:280
  19.5 0.0 copy-done.1
  19.5 2.1 %pad.15 = bf16[3,3,640,192]{3,2,1,0:T(8,128)(2,1)} pad(bf16[3,3,576,192]{3,2,1,0:T(8,128)(2,1)S(1)} %bitcast.22, bf16[]{:T(256)} %constant.2.clone.1), padding=0_0x0_0x0_64x0_0 | pad | bytes 4202498 | tf_op jit(solution)/shard_map/jit(_pad)/pad | solution.py:280
  21.7 101.4 %shard_map.82 = bf16[4,1024,192]{2,1,0:T(8,128)(2,1)} custom-call(bf16[4,1024,192]{2,1,0:T(8,128)(2,1)} %bitcast.28, bf16[4,4096,96]{2,1,0:T(8,128)(2,1)} %bitcast.26, f32[1,192]{1,0:T(1,128)} %bitcast.29, f32[1,192]{1,0:T(1,128)} %bitcast.30, f32[1,192]{1,0:T(1,128)} %bitcast.31, bf16[1152,192]{1,0:T(8,128)(2,1)} %bitcast.27, ...), custom_call_target="tpu_custom_call" | custom-call | tf_op jit(solution)/shard_map/pallas_call | solution.py:291
  123.1 3.1 %copy.15 = bf16[4,32,32,192]{3,2,1,0:T(8,128)(2,1)} copy(bf16[4,32,32,192]{3,2,1,0:T(8,128)(2,1)} %bitcast.25) | data formatting | bytes 3145728
Async XLA Ops:
  7.7 4.0 %copy-start = (bf16[3,3,3,192,192]{4,3,2,1,0:T(8,128)(2,1)S(1)}, bf16[3,3,3,192,192]{4,3,2,1,0:T(8,128)(2,1)}, u32[]{:S(2)}) copy-start(bf16[3,3,3,192,192]{4,3,2,1,0:T(8,128)(2,1)} %param.9) | copy-start | bytes 5971972
  15.5 4.0 %copy-start.1 = (bf16[3,3,3,192,192]{4,3,2,1,0:T(8,128)(2,1)S(1)}, bf16[3,3,3,192,192]{4,3,2,1,0:T(8,128)(2,1)}, u32[]{:S(2)}) copy-start(bf16[3,3,3,192,192]{4,3,2,1,0:T(8,128)(2,1)} %param.9) | copy-start | bytes 5971972
where the time goes:
time: 127 us; the launch traced here: 126 us
  Pallas kernels  101 us (80%)
  local copies, waits for them, and re-layouts  24.7 us (19%)
    pallas_call x1, Pallas kernels, per_device(): pl.pallas_call(functools.partial(kernel, dims), out_shape=jax.ShapeDtypeS...  101 us
    pad x3, local copies, waits for them, and re-layouts, taps(): weight = jnp.pad(weight, ((0, 0), (0, 0), (0, wide - 3 * chans), (0, 0)))  10.1 us
    transpose x4, local copies, waits for them, and re-layouts, per_device(): flip = lambda w: jnp.flip(w, (0, 1, 2)).swapaxes(3, 4)  9.36 us
    unnamed x6, local copies, waits for them, and re-layouts  3.32 us

commit v1 on v0

v1 whole, which is shorter than its diff:
```python
import functools

import jax
import jax.numpy as jnp
from jax import lax
from jax.experimental import pallas as pl
from jax.experimental.pallas import tpu as pltpu
from jax.sharding import PartitionSpec as P

MESH = pl.DeviceIdType.MESH
F32, BF16 = jnp.float32, jnp.bfloat16
LEAD = 8
STEP = 16
FEW = 2


def rms_scale(value):
    return lax.rsqrt(jnp.mean(value * value, axis=-1, keepdims=True) + 1e-06)


def silu_slope(value):
    sig = jax.nn.sigmoid(value)
    return sig * (1.0 + value * (1.0 - sig))


def rms_back(value, scale, gain, grad):
    scaled = gain * grad
    return scale * scaled - value * scale**3 * jnp.mean(value * scaled, axis=-1, keepdims=True)


class Field:
    def __init__(self, ref, parts, one_frame, rows, cols):
        self.ref, self.parts, self.one_frame = ref, parts, one_frame
        self.rows, self.cols = rows, cols

    def part(self, t, h):
        return h if self.one_frame else t * self.parts + h

    def put(self, t, row, values):
        n = self.cols
        for h in range(self.parts):
            for r in range(values.shape[0] // n):
                self.ref[self.part(t, h), row + r + 1, pl.ds(LEAD, n), :] = values[
                    r * n : (r + 1) * n, h * 128 : (h + 1) * 128
                ]

    def line(self, t, row):
        return jnp.concatenate([self.ref[self.part(t, h), row, pl.ds(LEAD, self.cols), :] for h in range(self.parts)], axis=1)

    def get(self, t, row, count):
        return jnp.concatenate([self.line(t, row + r + 1) for r in range(count)], axis=0)

    def column(self, t, col):
        cells = [self.ref[self.part(t, h), pl.ds(1, self.rows), pl.ds(LEAD + col, 1), :] for h in range(self.parts)]
        return jnp.concatenate([c.reshape(self.rows, 128) for c in cells], axis=1)

    def take_edges(self, t, stage):
        stage[0, t] = self.line(t, 1).astype(BF16)
        stage[1, t] = self.line(t, self.rows).astype(BF16)
        stage[2, t] = self.column(t, 0).astype(BF16)
        stage[3, t] = self.column(t, self.cols - 1).astype(BF16)

    def set_edges(self, t, hal, cor, inside):
        up, down, left, right = inside
        n, low = self.cols, self.rows + 1
        lines = [
            (0, LEAD, hal[0, t].astype(F32) * up),
            (low, LEAD, hal[1, t].astype(F32) * down),
            (0, LEAD - 1, cor[0, t].astype(F32)[15:16] * (up * left)),
            (0, LEAD + n, cor[1, t].astype(F32)[0:1] * (up * right)),
            (low, LEAD - 1, cor[2, t].astype(F32)[15:16] * (down * left)),
            (low, LEAD + n, cor[3, t].astype(F32)[0:1] * (down * right)),
        ]
        columns = [
            (LEAD - 1, hal[2, t].astype(F32) * left),
            (LEAD + n, hal[3, t].astype(F32) * right),
        ]
        for h in range(self.parts):
            lanes = slice(h * 128, (h + 1) * 128)
            for row, at, values in lines:
                self.ref[self.part(t, h), row, pl.ds(at, values.shape[0]), :] = values[:, lanes]
            for at, values in columns:
                self.ref[self.part(t, h), pl.ds(1, self.rows), pl.ds(at, 1), :] = values[:, lanes].reshape(self.rows, 1, 128)


def kernel(
    dims, feats, cot, bias_first, gain_first, gain_second, up_weight, first_hbm, second_hbm, out,
    g0, g1, x0, x1, cf, boxes, pre, acc, wu, w1, w2, w3, raw, stage, hal, cor, cstage, chal, ccor,
    w_sem, send, recv,
):
    count_h, count_w, frames, rows, cols, chans, fine_chans = dims
    me_h, me_w = lax.axis_index("ha"), lax.axis_index("wa")
    up, down = lax.rem(me_h + count_h - 1, count_h), lax.rem(me_h + 1, count_h)
    left, right = lax.rem(me_w + count_w - 1, count_w), lax.rem(me_w + 1, count_w)
    inside = [
        jnp.where(has, 1.0, 0.0).astype(F32)
        for has in (me_h > 0, me_h < count_h - 1, me_w > 0, me_w < count_w - 1)
    ]
    peers = [
        (up, me_w), (down, me_w), (me_h, left), (me_h, right),
        (up, left), (up, right), (down, left), (down, right),
    ]
    barrier = pltpu.get_barrier_semaphore()
    for peer in peers:
        pl.semaphore_signal(barrier, inc=1, device_id=peer, device_id_type=MESH)

    load_first = pltpu.make_async_copy(first_hbm, raw, w_sem.at[0])
    load_second = pltpu.make_async_copy(second_hbm, raw, w_sem.at[1])
    load_first.start()
    wide = x0.shape[-1]

    def place(weight, adjoint):
        @pl.loop(0, 9)
        def _(i):
            base = pl.multiple_of(i * wide, 128)
            for q in range(3):
                tap = raw[26 - (3 * i + q)].T if adjoint else raw[3 * i + q]
                weight[pl.ds(base + q * 128, 128), :] = tap[:128]
                weight[pl.ds(base + 384 + q * 64, 64), :] = tap[128:]
            weight[pl.ds(base + 576, 64), :] = jnp.zeros((64, chans), BF16)

    def exchange(stage, hal, cor, sem, t=None):
        at = (slice(None),) if t is None else (t,)
        n = stage.shape[2]
        first, last = pl.ds(0, 16), pl.ds(n - 16, 16)
        routes = [
            (stage.at[(0, *at)], hal.at[(1, *at)]),
            (stage.at[(1, *at)], hal.at[(0, *at)]),
            (stage.at[(2, *at)], hal.at[(3, *at)]),
            (stage.at[(3, *at)], hal.at[(2, *at)]),
            (stage.at[(0, *at, first)], cor.at[(3, *at)]),
            (stage.at[(0, *at, last)], cor.at[(2, *at)]),
            (stage.at[(1, *at, first)], cor.at[(1, *at)]),
            (stage.at[(1, *at, last)], cor.at[(0, *at)]),
        ]
        copies = [
            pltpu.make_async_remote_copy(
                src_ref=src, dst_ref=dst, send_sem=send.at[sem, i], recv_sem=recv.at[sem, i],
                device_id=peer, device_id_type=MESH,
            )
            for i, ((src, dst), peer) in enumerate(zip(routes, peers))
        ]
        for copy in copies:
            copy.start()
        return copies

    def arrive(copies):
        for copy in copies:
            copy.wait()

    active = Field(g0, 2, False, rows, cols)
    block = Field(g1, 2, False, rows, cols)
    fine = Field(cf, 1, True, 2 * rows, 2 * cols)
    span = STEP * cols

    def over_rows(body):
        @pl.loop(0, rows // STEP)
        def _(c):
            body(c * STEP, pl.ds(pl.multiple_of(c * span, span), span))

    def over_cells(count, body):
        size = FEW * cols

        @pl.loop(0, count // FEW, unroll=2)
        def _(c):
            body(c * FEW, pl.ds(pl.multiple_of(c * size, size), size))

    zero_lanes = jnp.zeros((2 * cols, 128 - fine_chans), F32)

    def load_fine(t):
        @pl.loop(0, 2 * rows, unroll=8)
        def _(y):
            cells = cot[t, pl.ds(pl.multiple_of(y * 2 * cols, 2 * cols), 2 * cols), :].astype(F32)
            fine.put(t, y, jnp.concatenate([cells, zero_lanes], axis=1))

    for t in range(frames):
        load_fine(t)
        fine.take_edges(t, cstage)
    pl.semaphore_wait(barrier, len(peers))
    cot_sent = exchange(cstage, chal, ccor, 0)

    def pad_lanes(values):
        return jnp.concatenate([values, jnp.zeros((values.shape[0], 256 - chans), F32)], axis=1)

    for t in range(frames):
        def first_norm(row, at, t=t):
            value = feats[t, at, :].astype(F32)
            normed = value * rms_scale(value) * gain_first[...]
            active.put(t, row, pad_lanes(normed * jax.nn.sigmoid(normed)))
        over_cells(rows, first_norm)
        active.take_edges(t, stage.at[0])
    active_sent = exchange(stage.at[0], hal.at[0], cor.at[0], 1)

    load_first.wait()
    place(w1, False)
    place(w3, True)
    load_second.start()
    for i in range(9):
        wu[pl.ds(i * 128, fine_chans), :] = up_weight[8 - i].T
        wu[pl.ds(i * 128 + fine_chans, 128 - fine_chans), :] = jnp.zeros((128 - fine_chans, chans), BF16)

    arrive(cot_sent)
    for t in range(frames):
        load_fine(t)
        fine.set_edges(t, chal, ccor, inside)

        @pl.loop(0, rows, unroll=2)
        def _(row):
            def pairs(y):
                before, even, odd, after = [
                    cf[0, y, pl.ds(LEAD + d, cols, stride=2), :] for d in (-1, 0, 1, 2)
                ]
                return [before + even, even + odd, odd + after]

            sums = [pairs(2 * row + d) for d in range(4)]
            at = pl.ds(pl.multiple_of(row * cols, cols), cols)
            for a in range(3):
                for b in range(3):
                    boxes[at, pl.ds((3 * a + b) * 128, 128)] = (sums[a][b] + sums[a + 1][b]).astype(BF16)

        def coarse(row, at, t=t):
            block.put(t, row, pad_lanes(jnp.dot(boxes[at, :], wu[...], preferred_element_type=F32)))

        over_rows(coarse)
        block.take_edges(t, stage.at[1])
    block_sent = exchange(stage.at[1], hal.at[1], cor.at[1], 2)
    load_second.wait()
    place(w2, True)

    def widen(field, t, x):
        @pl.loop(0, rows + 2, unroll=2)
        def _(row):
            main, rest = [
                [field.ref[field.part(t, h), row, pl.ds(LEAD + d, cols), :] for d in (-1, 0, 1)] for h in range(2)
            ]
            both = jnp.concatenate([rest[0][:, :64], rest[1][:, :64]], axis=1)
            at = pl.ds(pl.multiple_of(row * cols, cols), cols)
            for i, cells in enumerate([*main, both, rest[2]]):
                x[t, at, pl.ds(i * 128, 128)] = cells.astype(BF16)

    def conv(x, weight, first, sources, row):
        lhs = jnp.concatenate(
            [x[t, pl.ds(pl.multiple_of((row + p) * cols, cols), span), :] for t in sources for p in range(3)], axis=1
        )
        rhs = weight[pl.ds(first * 3 * wide, len(sources) * 3 * wide), :]
        return jnp.dot(lhs, rhs, preferred_element_type=F32)

    arrive(active_sent)
    for t in range(frames):
        active.set_edges(t, hal.at[0], cor.at[0], inside)
        widen(active, t, x0)

        def first_conv(row, at, t=t):
            first = max(0, 2 - t)
            pre[t, at, :] = conv(x0, w1, first, [t - 2 + k for k in range(first, 3)], row) + bias_first[...]

        over_rows(first_conv)

    arrive(block_sent)
    pre_sent = [None] * frames
    for t in reversed(range(frames)):
        block.set_edges(t, hal.at[1], cor.at[1], inside)
        widen(block, t, x1)

        def second_conv(row, at, t=t):
            acc[at, :] = conv(x1, w2, 0, range(t, min(t + 3, frames)), row)

        def second_norm(row, at, t=t):
            value = pre[t, at, :]
            scale = rms_scale(value)
            grad = acc[at, :] * silu_slope(value * scale * gain_second[...])
            active.put(t, row, pad_lanes(rms_back(value, scale, gain_second[...], grad)))

        over_rows(second_conv)
        over_cells(rows, second_norm)
        active.take_edges(t, stage.at[2])
        pre_sent[t] = exchange(stage.at[2], hal.at[2], cor.at[2], 3 + t, t)

    for t in reversed(range(frames)):
        arrive(pre_sent[t])
        active.set_edges(t, hal.at[2], cor.at[2], inside)
        widen(active, t, x0)

        def third_conv(row, at, t=t):
            acc[at, :] = conv(x0, w3, 0, range(t, min(t + 3, frames)), row)

        def third_norm(row, at, t=t):
            value = feats[t, at, :].astype(F32)
            scale = rms_scale(value)
            grad = acc[at, :] * silu_slope(value * scale * gain_first[...])
            through = rms_back(value, scale, gain_first[...], grad)
            out[t, at, :] = (block.get(t, row, FEW)[:, :chans] + through).astype(BF16)

        over_rows(third_conv)
        over_cells(rows, third_norm)


def per_device(
    count_h, count_w, features, conv_first, bias_first, gain_first, conv_second, gain_second, up_weight, cotangent
):
    frames, rows, cols, chans = features.shape
    fine_chans = cotangent.shape[-1]
    wide = -(-3 * chans // 128) * 128

    pitch, fine_pitch = cols + 16, 2 * cols + 16
    vmem, hbm = pl.BlockSpec(memory_space=pltpu.VMEM), pl.BlockSpec(memory_space=pl.ANY)
    dims = (count_h, count_w, frames, rows, cols, chans, fine_chans)
    field = pltpu.VMEM((2 * frames, rows + 2, pitch, 128), F32)
    spread = pltpu.VMEM((frames, (rows + 2) * cols, wide), BF16)
    weights = pltpu.VMEM((9 * wide, chans), BF16)
    out = pl.pallas_call(
        functools.partial(kernel, dims),
        out_shape=jax.ShapeDtypeStruct((frames, rows * cols, chans), BF16),
        in_specs=[vmem] * 6 + [hbm] * 2,
        out_specs=vmem,
        scratch_shapes=[
            field, field, spread, spread,
            pltpu.VMEM((1, 2 * rows + 2, fine_pitch, 128), F32),
            pltpu.VMEM((rows * cols, 9 * 128), BF16),
            pltpu.VMEM((frames, rows * cols, chans), F32),
            pltpu.VMEM((rows * cols, chans), F32),
            pltpu.VMEM((9 * 128, chans), BF16),
            weights, weights, weights,
            pltpu.VMEM((27, chans, chans), BF16),
            pltpu.VMEM((3, 4, frames, cols, 256), BF16),
            pltpu.VMEM((3, 4, frames, cols, 256), BF16),
            pltpu.VMEM((3, 4, frames, 16, 256), BF16),
            pltpu.VMEM((4, frames, 2 * cols, 128), BF16),
            pltpu.VMEM((4, frames, 2 * cols, 128), BF16),
            pltpu.VMEM((4, frames, 16, 128), BF16),
            pltpu.SemaphoreType.DMA((2,)),
            pltpu.SemaphoreType.DMA((3 + frames, 8)),
            pltpu.SemaphoreType.DMA((3 + frames, 8)),
        ],
        compiler_params=pltpu.CompilerParams(
            collective_id=0, has_side_effects=True, vmem_limit_bytes=60 * 2**20
        ),
    )(
        features.reshape(frames, rows * cols, chans),
        cotangent.reshape(frames, 4 * rows * cols, fine_chans),
        bias_first[None], gain_first[None], gain_second[None],
        up_weight.reshape(9, chans, fine_chans),
        conv_first.reshape(27, chans, chans), conv_second.reshape(27, chans, chans),
    )
    return out.reshape(frames, rows, cols, chans)


def solution(mesh):
    placed = (P(None, "ha", "wa", None), P(), P(), P(), P(), P(), P(), P(None, "ha", "wa", None))
    body = functools.partial(per_device, mesh.shape["ha"], mesh.shape["wa"])
    return jax.shard_map(body, mesh=mesh, in_specs=placed, out_specs=P(None, "ha", "wa", None), check_vma=False)
```

time: 127 us -> 94.1 us (0.74)
  local copies, waits for them, and re-layouts: 24.7 us -> 3.08 us
  Pallas kernels: 101 us -> 90.9 us
    pad x4 -> x0, local copies, waits for them, and re-layouts: 11 us -> none  [the longest x3 10.1 us: taps(): weight = jnp.pad(weight, ((0, 0), (0, 0), (0, wide - 3 * chans), (0, 0)))]
    pallas_call x1, Pallas kernels: 101 us -> 90.9 us  [per_device(): pl.pallas_call(functools.partial(kernel, dims), out_shape=jax.ShapeDtypeS...]
    transpose x5 -> x0, local copies, waits for them, and re-layouts: 10.4 us -> none  [the longest x4 9.36 us: per_device(): flip = lambda w: jnp.flip(w, (0, 1, 2)).swapaxes(3, 4)]
    unnamed x6 -> x1, local copies, waits for them, and re-layouts: 3.32 us -> 3.08 us
where the time goes in v1:
time: 94.1 us; the launch traced here: 94 us
  Pallas kernels  90.9 us (97%)
  local copies, waits for them, and re-layouts  3.08 us (3%)
    pallas_call x1, Pallas kernels, per_device(): pl.pallas_call(functools.partial(kernel, dims), out_shape=jax.ShapeDtypeS...  90.9 us
    unnamed x1, local copies, waits for them, and re-layouts  3.08 us

profile of v1, /device:TPU:0, one launch (start us, length us, event | category | flops | bytes accessed | tf_op | source)
XLA Modules:
  0.0 94.0 jit_solution(3965289783727091981)
XLA Ops:
  0.0 90.9 %shard_map.82 = bf16[4,1024,192]{2,1,0:T(8,128)(2,1)} custom-call(bf16[4,1024,192]{2,1,0:T(8,128)(2,1)} %bitcast.13, bf16[4,4096,96]{2,1,0:T(8,128)(2,1)} %bitcast.10, f32[1,192]{1,0:T(1,128)} %bitcast.15, f32[1,192]{1,0:T(1,128)} %bitcast.16, f32[1,192]{1,0:T(1,128)} %bitcast.17, bf16[9,192,96]{2,1,0:T(8,128)(2,1)} %bitcast.14, ...), custom_call_target="tpu_custom_call" | custom-call | tf_op jit(solution)/shard_map/pallas_call | solution.py:311
  90.9 3.1 %copy.10 = bf16[4,32,32,192]{3,2,1,0:T(8,128)(2,1)} copy(bf16[4,32,32,192]{3,2,1,0:T(8,128)(2,1)} %bitcast.9) | data formatting | bytes 3145728

commit v2 on v1

--- a/solution.py
+++ b/solution.py
@@ -26,6 +26,10 @@
 def rms_back(value, scale, gain, grad):
     scaled = gain * grad
     return scale * scaled - value * scale**3 * jnp.mean(value * scaled, axis=-1, keepdims=True)
+
+
+def multiple(index, of):
+    return index if isinstance(index, int) else pl.multiple_of(index, of)
 
 
 class Field:
@@ -85,7 +89,7 @@
 
 def kernel(
     dims, feats, cot, bias_first, gain_first, gain_second, up_weight, first_hbm, second_hbm, out,
-    g0, g1, x0, x1, cf, boxes, pre, acc, wu, w1, w2, w3, raw, stage, hal, cor, cstage, chal, ccor,
+    g0, g1, x0, x1, x2, x3, y0, y1, y2, y3, cf, boxes, pre, acc0, acc1, wu, w1, w2, raw1, raw2, stage, hal, cor, cstage, chal, ccor,
     w_sem, send, recv,
 ):
     count_h, count_w, frames, rows, cols, chans, fine_chans = dims
@@ -104,20 +108,20 @@
     for peer in peers:
         pl.semaphore_signal(barrier, inc=1, device_id=peer, device_id_type=MESH)
 
-    load_first = pltpu.make_async_copy(first_hbm, raw, w_sem.at[0])
-    load_second = pltpu.make_async_copy(second_hbm, raw, w_sem.at[1])
+    load_first = pltpu.make_async_copy(first_hbm, raw1, w_sem.at[0])
+    load_second = pltpu.make_async_copy(second_hbm, raw2, w_sem.at[1])
     load_first.start()
+    load_second.start()
+    xs, ys = (x0, x1, x2, x3), (y0, y1, y2, y3)
     wide = x0.shape[-1]
 
-    def place(weight, adjoint):
-        @pl.loop(0, 9)
-        def _(i):
-            base = pl.multiple_of(i * wide, 128)
-            for q in range(3):
-                tap = raw[26 - (3 * i + q)].T if adjoint else raw[3 * i + q]
-                weight[pl.ds(base + q * 128, 128), :] = tap[:128]
-                weight[pl.ds(base + 384 + q * 64, 64), :] = tap[128:]
-            weight[pl.ds(base + 576, 64), :] = jnp.zeros((64, chans), BF16)
+    def place(weight, raw, i, adjoint):
+        base = multiple(i * wide, 128)
+        for q in range(3):
+            tap = raw[26 - (3 * i + q)].T if adjoint else raw[3 * i + q]
+            weight[pl.ds(base + q * 128, 128), :] = tap[:128]
+            weight[pl.ds(base + 384 + q * 64, 64), :] = tap[128:]
+        weight[pl.ds(base + 576, 64), :] = jnp.zeros((64, chans), BF16)
 
     def exchange(stage, hal, cor, sem, t=None):
         at = (slice(None),) if t is None else (t,)
@@ -192,9 +196,11 @@
     active_sent = exchange(stage.at[0], hal.at[0], cor.at[0], 1)
 
     load_first.wait()
-    place(w1, False)
-    place(w3, True)
-    load_second.start()
+
+    @pl.loop(0, 9)
+    def _(i):
+        place(w1, raw1, i, False)
+
     for i in range(9):
         wu[pl.ds(i * 128, fine_chans), :] = up_weight[8 - i].T
         wu[pl.ds(i * 128 + fine_chans, 128 - fine_chans), :] = jnp.zeros((128 - fine_chans, chans), BF16)
@@ -204,19 +210,22 @@
         load_fine(t)
         fine.set_edges(t, chal, ccor, inside)
 
-        @pl.loop(0, rows, unroll=2)
-        def _(row):
+        @pl.loop(0, rows // 4)
+        def _(c):
             def pairs(y):
                 before, even, odd, after = [
                     cf[0, y, pl.ds(LEAD + d, cols, stride=2), :] for d in (-1, 0, 1, 2)
                 ]
                 return [before + even, even + odd, odd + after]
 
-            sums = [pairs(2 * row + d) for d in range(4)]
-            at = pl.ds(pl.multiple_of(row * cols, cols), cols)
-            for a in range(3):
-                for b in range(3):
-                    boxes[at, pl.ds((3 * a + b) * 128, 128)] = (sums[a][b] + sums[a + 1][b]).astype(BF16)
+            sums = [pairs(8 * c + d) for d in range(10)]
+            for r in range(4):
+                at = pl.ds(pl.multiple_of((4 * c + r) * cols, cols), cols)
+                for a in range(3):
+                    for b in range(3):
+                        boxes[at, pl.ds((3 * a + b) * 128, 128)] = (
+                            sums[2 * r + a][b] + sums[2 * r + a + 1][b]
+                        ).astype(BF16)
 
         def coarse(row, at, t=t):
             block.put(t, row, pad_lanes(jnp.dot(boxes[at, :], wu[...], preferred_element_type=F32)))
@@ -225,74 +234,95 @@
         block.take_edges(t, stage.at[1])
     block_sent = exchange(stage.at[1], hal.at[1], cor.at[1], 2)
     load_second.wait()
-    place(w2, True)
-
-    def widen(field, t, x):
-        @pl.loop(0, rows + 2, unroll=2)
-        def _(row):
+
+    def widen(field, t, x, low, high):
+        for row in range(low, high):
             main, rest = [
                 [field.ref[field.part(t, h), row, pl.ds(LEAD + d, cols), :] for d in (-1, 0, 1)] for h in range(2)
             ]
             both = jnp.concatenate([rest[0][:, :64], rest[1][:, :64]], axis=1)
-            at = pl.ds(pl.multiple_of(row * cols, cols), cols)
             for i, cells in enumerate([*main, both, rest[2]]):
-                x[t, at, pl.ds(i * 128, 128)] = cells.astype(BF16)
+                x[pl.ds(row * cols, cols), pl.ds(i * 128, 128)] = cells.astype(BF16)
 
     def conv(x, weight, first, sources, row):
-        lhs = jnp.concatenate(
-            [x[t, pl.ds(pl.multiple_of((row + p) * cols, cols), span), :] for t in sources for p in range(3)], axis=1
-        )
+        lhs = jnp.concatenate([x[t][pl.ds((row + p) * cols, span), :] for t in sources for p in range(3)], axis=1)
         rhs = weight[pl.ds(first * 3 * wide, len(sources) * 3 * wide), :]
         return jnp.dot(lhs, rhs, preferred_element_type=F32)
 
-    arrive(active_sent)
-    for t in range(frames):
-        active.set_edges(t, hal.at[0], cor.at[0], inside)
-        widen(active, t, x0)
-
-        def first_conv(row, at, t=t):
-            first = max(0, 2 - t)
-            pre[t, at, :] = conv(x0, w1, first, [t - 2 + k for k in range(first, 3)], row) + bias_first[...]
-
-        over_rows(first_conv)
-
-    arrive(block_sent)
-    pre_sent = [None] * frames
-    for t in reversed(range(frames)):
-        block.set_edges(t, hal.at[1], cor.at[1], inside)
-        widen(block, t, x1)
-
-        def second_conv(row, at, t=t):
-            acc[at, :] = conv(x1, w2, 0, range(t, min(t + 3, frames)), row)
-
-        def second_norm(row, at, t=t):
-            value = pre[t, at, :]
+    def first_conv(t, row, acc):
+        first = max(0, 2 - t)
+        at = pl.ds(row * cols, span)
+        pre[t, at, :] = conv(xs, w1, first, [t - 2 + k for k in range(first, 3)], row) + bias_first[...]
+
+    def second_conv(t, row, acc):
+        acc[...] = conv(ys, w2, 0, range(t, min(t + 3, frames)), row)
+
+    def third_conv(t, row, acc):
+        acc[...] = conv(xs, w1, 0, range(t, min(t + 3, frames)), row)
+
+    def second_norm(t, row, acc):
+        for r in range(0, STEP, FEW):
+            value = pre[t, pl.ds((row + r) * cols, FEW * cols), :]
             scale = rms_scale(value)
-            grad = acc[at, :] * silu_slope(value * scale * gain_second[...])
-            active.put(t, row, pad_lanes(rms_back(value, scale, gain_second[...], grad)))
-
-        over_rows(second_conv)
-        over_cells(rows, second_norm)
-        active.take_edges(t, stage.at[2])
-        pre_sent[t] = exchange(stage.at[2], hal.at[2], cor.at[2], 3 + t, t)
-
-    for t in reversed(range(frames)):
-        arrive(pre_sent[t])
-        active.set_edges(t, hal.at[2], cor.at[2], inside)
-        widen(active, t, x0)
-
-        def third_conv(row, at, t=t):
-            acc[at, :] = conv(x0, w3, 0, range(t, min(t + 3, frames)), row)
-
-        def third_norm(row, at, t=t):
+            grad = acc[pl.ds(r * cols, FEW * cols), :] * silu_slope(value * scale * gain_second[...])
+            active.put(t, row + r, pad_lanes(rms_back(value, scale, gain_second[...], grad)))
+
+    def third_norm(t, row, acc):
+        for r in range(0, STEP, FEW):
+            at = pl.ds((row + r) * cols, FEW * cols)
             value = feats[t, at, :].astype(F32)
             scale = rms_scale(value)
-            grad = acc[at, :] * silu_slope(value * scale * gain_first[...])
+            grad = acc[pl.ds(r * cols, FEW * cols), :] * silu_slope(value * scale * gain_first[...])
             through = rms_back(value, scale, gain_first[...], grad)
-            out[t, at, :] = (block.get(t, row, FEW)[:, :chans] + through).astype(BF16)
-
-        over_rows(third_conv)
-        over_cells(rows, third_norm)
+            out[t, at, :] = (block.get(t, row + r, FEW)[:, :chans] + through).astype(BF16)
+
+    arrive(active_sent)
+    active.set_edges(0, hal.at[0], cor.at[0], inside)
+    widen(active, 0, x0, 0, rows + 2)
+
+    halves = rows // STEP
+    order = [("first", t, c) for t in range(frames) for c in range(halves)]
+    order += [(stage_of, t, c) for stage_of in ("second", "third") for t in reversed(range(frames)) for c in range(halves)]
+    convs = {"first": first_conv, "second": second_conv, "third": third_conv}
+    norms = {"second": second_norm, "third": third_norm}
+    pre_sent = [None] * frames
+    before = None
+    for count, (name, t, c) in enumerate(order):
+        if name == "first":
+            ahead = (active, t + 1, xs, 0) if t + 1 < frames else (block, frames - 1, ys, 1)
+        elif name == "second":
+            ahead = (block, t - 1, ys, 1) if t > 0 else (active, frames - 1, xs, 2)
+        else:
+            ahead = (active, t - 1, xs, 2) if t > 0 else None
+        if c == 0 and ahead is not None:
+            field, other, _, slot = ahead
+            if name == "first" and slot == 1:
+                arrive(block_sent)
+            if slot == 2:
+                arrive(pre_sent[other])
+            field.set_edges(other, hal.at[slot], cor.at[slot], inside)
+        taps_at = [i for i in range(9) if i * frames * halves // 9 == count % (frames * halves)]
+
+        @pl.when(me_h >= 0)
+        def _():
+            if before is not None:
+                norms[before[0]](before[1], before[2] * STEP, (acc0, acc1)[(count - 1) % 2])
+            convs[name](t, c * STEP, (acc0, acc1)[count % 2])
+            if ahead is not None:
+                share = (rows + 2) // halves
+                widen(ahead[0], ahead[1], ahead[2][ahead[1]], c * share, rows + 2 if c == halves - 1 else (c + 1) * share)
+            for i in taps_at:
+                if name == "first":
+                    place(w2, raw2, i, True)
+                if name == "second":
+                    place(w1, raw1, i, True)
+
+        if before is not None and before[0] == "second" and before[2] == halves - 1:
+            done = before[1]
+            active.take_edges(done, stage.at[2])
+            pre_sent[done] = exchange(stage.at[2], hal.at[2], cor.at[2], 3 + done, done)
+        before = (name, t, c) if name in norms else None
+    norms[before[0]](before[1], before[2] * STEP, (acc0, acc1)[(len(order) - 1) % 2])
 
 
 def per_device(
@@ -306,7 +336,7 @@
     vmem, hbm = pl.BlockSpec(memory_space=pltpu.VMEM), pl.BlockSpec(memory_space=pl.ANY)
     dims = (count_h, count_w, frames, rows, cols, chans, fine_chans)
     field = pltpu.VMEM((2 * frames, rows + 2, pitch, 128), F32)
-    spread = pltpu.VMEM((frames, (rows + 2) * cols, wide), BF16)
+    spread = [pltpu.VMEM(((rows + 2) * cols, wide), BF16)] * (2 * frames)
     weights = pltpu.VMEM((9 * wide, chans), BF16)
     out = pl.pallas_call(
         functools.partial(kernel, dims),
@@ -314,13 +344,15 @@
         in_specs=[vmem] * 6 + [hbm] * 2,
         out_specs=vmem,
         scratch_shapes=[
-            field, field, spread, spread,
+            field, field, *spread,
             pltpu.VMEM((1, 2 * rows + 2, fine_pitch, 128), F32),
             pltpu.VMEM((rows * cols, 9 * 128), BF16),
             pltpu.VMEM((frames, rows * cols, chans), F32),
-            pltpu.VMEM((rows * cols, chans), F32),
+            pltpu.VMEM((STEP * cols, chans), F32),
+            pltpu.VMEM((STEP * cols, chans), F32),
             pltpu.VMEM((9 * 128, chans), BF16),
-            weights, weights, weights,
+            weights, weights,
+            pltpu.VMEM((27, chans, chans), BF16),
             pltpu.VMEM((27, chans, chans), BF16),
             pltpu.VMEM((3, 4, frames, cols, 256), BF16),
             pltpu.VMEM((3, 4, frames, cols, 256), BF16),

time: 94.1 us -> 64 us (0.68)
  Pallas kernels: 90.9 us -> 60.8 us
    pallas_call x1, Pallas kernels: 90.9 us -> 60.8 us  [per_device(): pl.pallas_call(functools.partial(kernel, dims), out_shape=jax.ShapeDtypeS...]
where the time goes in v2:
time: 64 us; the launch traced here: 63.8 us
  Pallas kernels  60.8 us (95%)
  local copies, waits for them, and re-layouts  3.08 us (5%)
    pallas_call x1, Pallas kernels, per_device(): pl.pallas_call(functools.partial(kernel, dims), out_shape=jax.ShapeDtypeS...  60.8 us
    unnamed x1, local copies, waits for them, and re-layouts  3.08 us

profile of v2, /device:TPU:0, one launch (start us, length us, event | category | flops | bytes accessed | tf_op | source)
XLA Modules:
  0.0 63.8 jit_solution(7477094371432755824)
XLA Ops:
  0.0 60.8 %shard_map.82 = bf16[4,1024,192]{2,1,0:T(8,128)(2,1)} custom-call(bf16[4,1024,192]{2,1,0:T(8,128)(2,1)} %bitcast.13, bf16[4,4096,96]{2,1,0:T(8,128)(2,1)} %bitcast.10, f32[1,192]{1,0:T(1,128)} %bitcast.15, f32[1,192]{1,0:T(1,128)} %bitcast.16, f32[1,192]{1,0:T(1,128)} %bitcast.17, bf16[9,192,96]{2,1,0:T(8,128)(2,1)} %bitcast.14, ...), custom_call_target="tpu_custom_call" | custom-call | tf_op jit(solution)/shard_map/pallas_call | solution.py:341
  60.8 3.1 %copy.10 = bf16[4,32,32,192]{3,2,1,0:T(8,128)(2,1)} copy(bf16[4,32,32,192]{3,2,1,0:T(8,128)(2,1)} %bitcast.9) | data formatting | bytes 3145728

commit v3 on v2

--- a/solution.py
+++ b/solution.py
@@ -165,7 +165,7 @@
     def over_cells(count, body):
         size = FEW * cols
 
-        @pl.loop(0, count // FEW, unroll=2)
+        @pl.loop(0, count // FEW, unroll=4)
         def _(c):
             body(c * FEW, pl.ds(pl.multiple_of(c * size, size), size))
 
@@ -177,8 +177,19 @@
             cells = cot[t, pl.ds(pl.multiple_of(y * 2 * cols, 2 * cols), 2 * cols), :].astype(F32)
             fine.put(t, y, jnp.concatenate([cells, zero_lanes], axis=1))
 
+    def load_border(t):
+        length = 2 * cols
+        for y in (0, 2 * rows - 1):
+            fine.put(t, y, jnp.concatenate([cot[t, pl.ds(y * length, length), :].astype(F32), zero_lanes], axis=1))
+
+        @pl.loop(0, 2 * rows, unroll=8)
+        def _(y):
+            for side in (0, length - 16):
+                cells = cot[t, pl.ds(pl.multiple_of(y * length, length) + side, 16), :].astype(F32)
+                cf[0, y + 1, pl.ds(LEAD + side, 16), :] = jnp.concatenate([cells, zero_lanes[:16]], axis=1)
+
     for t in range(frames):
-        load_fine(t)
+        load_border(t)
         fine.take_edges(t, cstage)
     pl.semaphore_wait(barrier, len(peers))
     cot_sent = exchange(cstage, chal, ccor, 0)
@@ -210,7 +221,7 @@
         load_fine(t)
         fine.set_edges(t, chal, ccor, inside)
 
-        @pl.loop(0, rows // 4)
+        @pl.loop(0, rows // 4, unroll=2)
         def _(c):
             def pairs(y):
                 before, even, odd, after = [

time: 64 us -> 64.5 us (level)
  no operation moved by 1% of the time
where the time goes in v3:
time: 64.5 us; the launch traced here: 64.3 us
  Pallas kernels  61.2 us (95%)
  local copies, waits for them, and re-layouts  3.08 us (5%)
    pallas_call x1, Pallas kernels, per_device(): pl.pallas_call(functools.partial(kernel, dims), out_shape=jax.ShapeDtypeS...  61.2 us
    unnamed x1, local copies, waits for them, and re-layouts  3.08 us

profile of v3, /device:TPU:0, one launch (start us, length us, event | category | flops | bytes accessed | tf_op | source)
XLA Modules:
  0.0 64.3 jit_solution(4251585219574398831)
XLA Ops:
  0.0 61.2 %shard_map.82 = bf16[4,1024,192]{2,1,0:T(8,128)(2,1)} custom-call(bf16[4,1024,192]{2,1,0:T(8,128)(2,1)} %bitcast.13, bf16[4,4096,96]{2,1,0:T(8,128)(2,1)} %bitcast.10, f32[1,192]{1,0:T(1,128)} %bitcast.15, f32[1,192]{1,0:T(1,128)} %bitcast.16, f32[1,192]{1,0:T(1,128)} %bitcast.17, bf16[9,192,96]{2,1,0:T(8,128)(2,1)} %bitcast.14, ...), custom_call_target="tpu_custom_call" | custom-call | tf_op jit(solution)/shard_map/pallas_call | solution.py:352
  61.2 3.1 %copy.10 = bf16[4,32,32,192]{3,2,1,0:T(8,128)(2,1)} copy(bf16[4,32,32,192]{3,2,1,0:T(8,128)(2,1)} %bitcast.9) | data formatting | bytes 3145728
